TPU v7x, 32 devices: a whole 2x2x4 slice. The times are simulated.
32 devices in a mesh: grp: 2 (over x), img: 16 (over z, y, core).
Axes of the slice: x: 2, y: 2, z: 4, core: 2. Of those that a mesh axis runs over, the one named last changes fastest.
Arguments:
- images: bfloat16 [2048, 3200], P(('grp', 'img')), parts along dimension 0, may hold values from -40 to 40
- projections: bfloat16 [32768, 3200], P(('grp', 'img')), parts along dimension 0, may hold values from -0.21875 to 0.21875
- noise_weight: float32 [6400], P('grp'), parts along dimension 0, may hold values from 0.3 to 3
- owners: int32 [2048, 4], P(('grp', 'img')), parts along dimension 0, may hold values from 0 to 15, all different within a row; in each aligned block of 64 rows (0 to 63, 64 to 127, ...) at most 32 rows name the same one
- counts: int32 [2048], P(('grp', 'img')), parts along dimension 0, may hold values from 2 to 4
Outputs:
- backproj: bfloat16 [32768, 3200], P(('grp', 'img')), parts along dimension 0
- weight_sum: float32 [32768], P(('grp', 'img')), parts along dimension 0
- loglik: float32 [2048], P(('grp', 'img')), parts along dimension 0
There are 2 independent parts, one for each index of `grp`. A program takes and returns all parts, laid end to end along the dimension named above; each array names one. Nothing has to cross between parts.
Inputs may be any that keep to these rules, and one draw needn't show every extreme that they name: `owners`: the 4 blocks named in a row differ; among the rows of one device's 64 images no block is named more than 32 times, and some block is named exactly 32 times. Only the first counts[i] entries of row i of owners are live.
All inputs are finite; a program needn't handle non-finite values.
Results may differ from a plain program's by a relative error of at most 0.001.
The roundings to bfloat16 on the way count: a program that leaves them out, or rounds other values in their place, can miss the bound.
Values may be sent and summed in bfloat16 or wider, within the bound.
A program may use at most 64 MiB of HBM per device.

v0:
```python
import jax
import jax.numpy as jnp
from jax import lax
from jax.sharding import PartitionSpec as P


def slot_layout(owners, devices, capacity):
    owner_flat = owners.reshape(-1)
    one_hot = (owner_flat[:, None] == jnp.arange(devices, dtype=jnp.int32)[None, :]).astype(
        jnp.int32
    )
    earlier = jnp.cumsum(one_hot, axis=0) - one_hot
    within = jnp.sum(earlier * one_hot, axis=1)
    return owner_flat * capacity + within


def shards(images, projections, noise_weight, owners, counts):
    devices = lax.axis_size("img")
    local_images, width = images.shape
    candidates = owners.shape[1]
    capacity = 2 * local_images * candidates // devices
    block_dirs = projections.shape[0]
    target = slot_layout(owners, devices, capacity)
    source_rows = jnp.repeat(jnp.arange(local_images, dtype=jnp.int32), candidates)
    outgoing = (
        jnp.zeros((devices * capacity, width), jnp.bfloat16).at[target].set(images[source_rows])
    )
    arrived = lax.all_to_all(
        outgoing.reshape(devices, capacity, width), "img", split_axis=0, concat_axis=0, tiled=True
    ).reshape(devices * capacity, width)
    proj_wide = projections.astype(jnp.float32)
    weighted = (proj_wide * noise_weight[None, :]).astype(jnp.bfloat16)
    power = jnp.sum(proj_wide * proj_wide * noise_weight[None, :], axis=1)
    scores = (
        lax.dot_general(
            arrived, weighted, (((1,), (1,)), ((), ())), preferred_element_type=jnp.float32
        )
        - 0.5 * power[None, :]
    )
    live_slot = jnp.arange(candidates, dtype=jnp.int32)[None, :] < counts[:, None]
    returned = lax.all_to_all(
        scores.reshape(devices, capacity, block_dirs),
        "img",
        split_axis=0,
        concat_axis=0,
        tiled=True,
    ).reshape(devices * capacity, block_dirs)
    mine = returned[target].reshape(local_images, candidates, block_dirs)
    peak_score = jnp.max(jnp.where(live_slot[:, :, None], mine, -jnp.inf), axis=(1, 2))
    shifted = jnp.where(live_slot[:, :, None], jnp.exp(mine - peak_score[:, None, None]), 0.0)
    sum_total = jnp.sum(shifted, axis=(1, 2))
    loglik = peak_score + jnp.log(sum_total)
    posterior = (shifted * (1.0 / sum_total)[:, None, None]).astype(jnp.bfloat16)
    outgoing_post = (
        jnp.zeros((devices * capacity, block_dirs), jnp.bfloat16)
        .at[target]
        .set(posterior.reshape(-1, block_dirs))
    )
    weights_here = lax.all_to_all(
        outgoing_post.reshape(devices, capacity, block_dirs),
        "img",
        split_axis=0,
        concat_axis=0,
        tiled=True,
    ).reshape(devices * capacity, block_dirs)
    backproj = lax.dot_general(
        weights_here, arrived, (((0,), (0,)), ((), ())), preferred_element_type=jnp.float32
    ).astype(jnp.bfloat16)
    weight_sum = jnp.sum(weights_here.astype(jnp.float32), axis=0)
    return (backproj, weight_sum, loglik)


def solution(mesh):
    in_specs = (
        P(("grp", "img"), None),
        P(("grp", "img"), None),
        P("grp"),
        P(("grp", "img"), None),
        P(("grp", "img")),
    )
    out_specs = (P(("grp", "img"), None), P(("grp", "img")), P(("grp", "img")))
    return jax.shard_map(shards, mesh=mesh, in_specs=in_specs, out_specs=out_specs, check_vma=False)
```

profile of v0, /device:TPU:0, one launch (start us, length us, event | category | flops | bytes accessed | tf_op | source)
XLA Modules:
  0.0 199.8 jit_solution(4020500099228161019)
XLA Ops:
  0.6 0.8 copy.9
  1.5 0.1 eq.29
  1.6 0.1 eq.25
  1.7 0.7 broadcast_multiply_fusion.1
  2.4 0.6 reduce-window.6
  3.0 0.2 slice_reduce_fusion
  3.2 0.1 copy.8
  3.3 0.1 mul.62
  3.4 0.1 reshape.141
  3.6 9.9 %scatter_custom_fusion = bf16[512,3200]{1,0:T(8,128)(2,1)} fusion(s32[256]{0:T(256)S(1)} %bitcast.36, bf16[64,3200]{1,0:T(8,128)(2,1)S(1)} %copy-done, s32[1024]{0:T(1024)S(1)} %pad_clamp_fusion.1, bf16[]{:T(256)} %constant.9.clone.1), kind=kCustom, calls=%fused_computation.13 | custom fusion | bytes 3276802 | tf_op jit(solution)/shard_map/scatter | solution.py:26
  13.6 7.6 %all-to-all-start = ((bf16[16,32,3200]{2,1,0:T(8,128)(2,1)}), bf16[16,32,3200]{2,1,0:T(8,128)(2,1)}, u32[]{:S(2)}, u32[]{:S(2)}) async-start(bf16[16,32,3200]{2,1,0:T(8,128)(2,1)} %bitcast.33), calls=%async_computation | async-start | bytes 6553600 | tf_op jit(solution)/shard_map/all_to_all | solution.py:28
  21.1 4.6 %fusion.2 = f32[1024]{0:T(1024)S(1)} fusion(bf16[1024,3200]{1,0:T(8,128)(2,1)} %param.6, f32[3200]{0:T(1024)S(1)} %copy-done.1), kind=kLoop, calls=%fused_computation.8 | loop fusion | flops 13106176 | bytes 6570496 | tf_op jit(solution)/shard_map/reduce_sum | solution.py:33
  25.8 57.1 %all-to-all-done = bf16[16,32,3200]{2,1,0:T(8,128)(2,1)} async-done(((bf16[16,32,3200]{2,1,0:T(8,128)(2,1)}), bf16[16,32,3200]{2,1,0:T(8,128)(2,1)}, u32[]{:S(2)}, u32[]{:S(2)}) %all-to-all-start) | async-done | bytes 3276832 | tf_op jit(solution)/shard_map/all_to_all | solution.py:28
  82.8 8.9 %fusion.9 = f32[512,1024]{1,0:T(8,128)} fusion(bf16[512,3200]{1,0:T(8,128)(2,1)} %bitcast.5, bf16[1024,3200]{1,0:T(8,128)(2,1)} %param.6, f32[3200]{0:T(1024)S(1)} %copy-done.1, f32[1024]{0:T(1024)S(1)} %broadcast_multiply_fusion), kind=kOutput, calls=%fused_computation.16 | convolution fusion | flops 3365797888 | bytes 11944448 | tf_op jit(solution)/shard_map/dot_general | solution.py:35
  91.7 16.1 %all-to-all-start.1 = ((f32[16,32,1024]{2,1,0:T(8,128)}), f32[16,32,1024]{2,1,0:T(8,128)S(1)}, u32[]{:S(2)}, u32[]{:S(2)}) async-start(f32[16,32,1024]{2,1,0:T(8,128)} %bitcast.35), calls=%async_computation.1 | async-start | bytes 4194304 | tf_op jit(solution)/shard_map/all_to_all | solution.py:41
  107.9 0.7 lt.46
  108.6 0.6 pad_clamp_fusion
  109.2 39.8 %all-to-all-done.1 = f32[16,32,1024]{2,1,0:T(8,128)S(1)} async-done(((f32[16,32,1024]{2,1,0:T(8,128)}), f32[16,32,1024]{2,1,0:T(8,128)S(1)}, u32[]{:S(2)}, u32[]{:S(2)}) %all-to-all-start.1) | async-done | bytes 2097184 | tf_op jit(solution)/shard_map/all_to_all | solution.py:41
  148.9 1.2 gather_fusion
  150.1 0.8 select_reduce_fusion
  151.0 0.1 reduce_max.14
  151.1 0.1 reduce_max.18
  151.3 0.1 sub.29
  151.4 1.0 fusion.12
  152.4 0.1 reduce_sum.49
  152.5 0.1 reduce_sum.50
  152.6 0.5 log_add_fusion
  153.2 0.1 mul.71
  153.3 2.2 %scatter_custom_fusion.1 = bf16[512,1024]{1,0:T(8,128)(2,1)S(1)} fusion(s32[256]{0:T(256)} %bitcast.38, f32[256,1024]{1,0:T(8,128)S(1)} %gather_fusion, f32[256]{0:T(256)S(1)} %mul.71, f32[]{:T(128)} %constant.5.clone.1, f32[256]{0:T(256)S(1)} %sub.29, bf16[]{:T(256)} %constant.9.clone.1, pred[256]{0:T(512)(128)(4,1)} %lt.46), kind=kCustom, calls=%fused_computation.21 | custom fusion | flops 1048576 | bytes 2100736 | tf_op jit(solution)/shard_map/scatter | solution.py:57
  155.6 35.9 %all_to_all.15 = bf16[16,32,1024]{2,1,0:T(8,128)(2,1)S(1)} all-to-all(bf16[16,32,1024]{2,1,0:T(8,128)(2,1)S(1)} %bitcast.34), channel_id=1, replica_groups=mesh['grp'=2,'img'=16] {'img'}, dimensions={0} | all-to-all | bytes 2097152 | tf_op jit(solution)/shard_map/all_to_all | solution.py:59
  191.4 7.6 %bitcast_convert_fusion = bf16[1024,3200]{1,0:T(8,128)(2,1)} fusion(bf16[16,32,1024]{2,1,0:T(8,128)(2,1)S(1)} %all_to_all.15, bf16[16,32,3200]{2,1,0:T(8,128)(2,1)} %all-to-all-done), kind=kOutput, calls=%fused_computation.9 | convolution fusion | flops 3358720000 | bytes 10878976 | tf_op jit(solution)/shard_map/dot_general | solution.py:66
  199.0 0.8 convert_reduce_fusion
  (20 shorter events, 0.4 us)
Async XLA Ops:
  0.6 3.0 %copy-start = (bf16[64,3200]{1,0:T(8,128)(2,1)S(1)}, bf16[64,3200]{1,0:T(8,128)(2,1)}, u32[]{:S(2)}) copy-start(bf16[64,3200]{1,0:T(8,128)(2,1)} %param.5) | copy-start | bytes 1228804
  3.6 104.9 %copy-start.2 = (s32[256,1]{0,1:T(1,128)}, s32[256,1]{0,1:T(1,128)S(1)}, u32[]{:S(2)}) copy-start(s32[256,1]{0,1:T(1,128)S(1)} %compare_select_fusion.1) | copy-start | bytes 3076
  13.6 7.6 %copy-start.1 = (f32[3200]{0:T(1024)S(1)}, f32[3200]{0:T(1024)}, u32[]{:S(2)}) copy-start(f32[3200]{0:T(1024)} %param.7) | copy-start | bytes 38404
  13.6 69.3 %all-to-all-start = ((bf16[16,32,3200]{2,1,0:T(8,128)(2,1)}), bf16[16,32,3200]{2,1,0:T(8,128)(2,1)}, u32[]{:S(2)}, u32[]{:S(2)}) async-start(bf16[16,32,3200]{2,1,0:T(8,128)(2,1)} %bitcast.33), calls=%async_computation | async-start | bytes 6553600 | tf_op jit(solution)/shard_map/all_to_all | solution.py:28
  91.7 16.1 %copy-start.3 = (s32[64]{0:T(128)S(1)}, s32[64]{0:T(128)}, u32[]{:S(2)}) copy-start(s32[64]{0:T(128)} %param.9) | copy-start | bytes 772
  91.7 57.2 %all-to-all-start.1 = ((f32[16,32,1024]{2,1,0:T(8,128)}), f32[16,32,1024]{2,1,0:T(8,128)S(1)}, u32[]{:S(2)}, u32[]{:S(2)}) async-start(f32[16,32,1024]{2,1,0:T(8,128)} %bitcast.35), calls=%async_computation.1 | async-start | bytes 4194304 | tf_op jit(solution)/shard_map/all_to_all | solution.py:41
where the time goes:
time: 201 us; the launch traced here: 200 us
  waiting for transfers between devices  96.8 us (48%)
  blocking collectives  35.9 us (18%)
  starting transfers between devices  23.7 us (12%)
  matrix products  16.5 us (8%)
  local copies, waits for them, and re-layouts  13.9 us (7%)
  other arithmetic  12.3 us (6%)
    all_to_all x1, waiting for transfers between devices, shards(): lax.all_to_all(outgoing.reshape(devices, capacity, width), 'img', split_a...  57.1 us
    all_to_all x1, waiting for transfers between devices, shards(): lax.all_to_all(scores.reshape(devices, capacity, block_dirs), 'img', spli...  39.8 us
    all_to_all x1, blocking collectives, shards(): lax.all_to_all(outgoing_post.reshape(devices, capacity, block_dirs), 'img...  35.9 us
    all_to_all x1, starting transfers between devices, shards(): lax.all_to_all(scores.reshape(devices, capacity, block_dirs), 'img', spli...  16.1 us
    scatter x1, local copies, waits for them, and re-layouts, shards(): jnp.zeros((devices * capacity, width), jnp.bfloat16).at[target]  9.91 us
    dot_general x1, matrix products, shards(): lax.dot_general(arrived, weighted, (((1,), (1,)), ((), ())), preferred_el...  8.89 us
    dot_general x1, matrix products, shards(): lax.dot_general(weights_here, arrived, (((0,), (0,)), ((), ())), preferre...  7.6 us
    all_to_all x1, starting transfers between devices, shards(): lax.all_to_all(outgoing.reshape(devices, capacity, width), 'img', split_a...  7.57 us
  transfers between devices with their start and end apart: 2, of which 2 were waited for; matrix products, arithmetic and copies ran while one was open for 3% of the time, Pallas kernels for 0%

commit v1 on v0

--- a/solution.py
+++ b/solution.py
@@ -1,7 +1,397 @@
 import jax
 import jax.numpy as jnp
 from jax import lax
+from jax.experimental import pallas as pl
+from jax.experimental.pallas import tpu as pltpu
 from jax.sharding import PartitionSpec as P
+
+NZ, NY, NC = 4, 2, 2
+PIECES = 2
+LOW = -1e30
+TILE_ROWS = 512
+
+
+def gather_and_score(
+    images, projections, noise, owners, counts,
+    gathered_out, post_out, wsum_out, loglik_out,
+    held, weighted, power, scores, post, stats, mask_out, mask_in, masks,
+    load_sem, own_sem, send_sem, recv_sem, store_sem, post_sem,
+    mask_send, mask_recv, stat_send, stat_recv,
+):
+    n = NZ * NY * NC
+    me = lax.axis_index("img")
+    z, y, c = me // (NY * NC), (me // NC) % NY, me % NC
+    rows = images.shape[0]
+    piece = rows // PIECES
+    block_dirs = projections.shape[0]
+    tiles = projections.shape[0] // 128
+    pair = NC * rows
+    chips = NZ * NY
+
+    def place(zs, ys, cs, h):
+        start = ((zs * NY + ys) * NC + cs) * rows + h * piece
+        return pl.ds(pl.multiple_of(start, piece), piece)
+
+    loads = [
+        pltpu.make_async_copy(
+            projections.at[pl.ds(t * 128, 128)], weighted.at[pl.ds(t * 128, 128)], load_sem.at[t]
+        )
+        for t in range(tiles)
+    ]
+    for load in loads:
+        load.start()
+    own_rows = pl.ds(pl.multiple_of(me * rows, rows), rows)
+    own_load = pltpu.make_async_copy(images, held.at[own_rows], own_sem)
+    own_load.start()
+
+    barrier = pltpu.get_barrier_semaphore()
+    peers = [lax.rem(me + k, n) for k in range(1, n)]
+    for peer in peers:
+        pl.semaphore_signal(barrier, inc=1, device_id={"img": peer})
+    pl.semaphore_wait(barrier, n - 1)
+
+    def copies(zs, same_line, h, own, toward):
+        ys = y if same_line else 1 - y
+        at = place(zs, ys, c, h)
+        src = images.at[pl.ds(h * piece, piece)] if own else held.at[at]
+        chip = zs * NY + ys
+        early = jnp.logical_or(zs == 0, zs == NZ - 1) if h == 1 else None
+
+        def copy(way, peer):
+            return pltpu.make_async_remote_copy(
+                src_ref=src, dst_ref=held.at[at], send_sem=send_sem.at[chip, h, way],
+                recv_sem=recv_sem.at[chip * NC + c, h], device_id={"img": peer},
+            )
+
+        out = []
+        line_ok = None if same_line else early
+        if same_line or early is not None:
+            for way, step in ((0, 1), (1, -1)):
+                if step in toward:
+                    ok = z < NZ - 1 if step == 1 else z > 0
+                    if line_ok is not None:
+                        ok = jnp.logical_and(ok, line_ok)
+                    out.append((ok, copy(way, me + step * NY * NC)))
+        if same_line:
+            if own or early is None:
+                ok = None
+            else:
+                ok = jnp.logical_not(early)
+            out.append((ok, copy(2, me + (1 - 2 * y) * NC)))
+        out.append((None, copy(3, me + 1 - 2 * c)))
+        return out
+
+    def act(items, do):
+        for ok, copy in items:
+            if ok is None:
+                do(copy)
+            else:
+                @pl.when(ok)
+                def _():
+                    do(copy)
+
+    def wait_arrival(zs, ys, cs, h):
+        at = place(zs, ys, cs, h)
+        pltpu.make_async_remote_copy(
+            src_ref=held.at[at], dst_ref=held.at[at], send_sem=send_sem.at[0, 0, 0],
+            recv_sem=recv_sem.at[(zs * NY + ys) * NC + cs, h], device_id={"img": me},
+        ).wait_recv()
+
+    def source(kind):
+        side, same_line, d = kind
+        zs = z + side * d
+        if d == 0:
+            return zs, None
+        return zs, (zs >= 0) if side < 0 else (zs <= NZ - 1)
+
+    def toward(kind):
+        side, same_line, d = kind
+        return (1, -1) if d == 0 else (-side,)
+
+    def guarded(ok, body):
+        if ok is None:
+            body()
+        else:
+            pl.when(ok)(body)
+
+    def relay(kind, h):
+        zs, ok = source(kind)
+
+        def body():
+            wait_arrival(zs, y if kind[1] else 1 - y, c, h)
+            act(copies(zs, kind[1], h, False, toward(kind)), lambda copy: copy.start())
+
+        guarded(ok, body)
+
+    def settle(kind, h, own):
+        zs, ok = source(kind)
+
+        def body():
+            act(copies(zs, kind[1], h, own, toward(kind)), lambda copy: copy.wait_send())
+
+        guarded(ok, body)
+
+    OWN = (0, True, 0)
+    for h in (1, 0):
+        act(copies(z, True, h, True, (1, -1)), lambda copy: copy.start())
+
+    lane = lax.broadcasted_iota(jnp.int32, (rows, 128), 1)
+    count = counts[...]
+    live = jnp.zeros((rows, 128), jnp.bool_)
+    for k in range(owners.shape[1]):
+        live = live | ((lane == owners[:, k:k + 1]) & (count > k))
+    spot = lax.broadcasted_iota(jnp.int32, (rows, 128), 0) + c * rows
+    pick = jnp.where(lane == spot, 1.0, 0.0)
+    by_owner = lax.dot_general(
+        jnp.where(live, 1.0, 0.0).astype(jnp.bfloat16), pick.astype(jnp.bfloat16),
+        (((0,), (0,)), ((), ())), preferred_element_type=jnp.float32,
+    )
+    for o in range(n):
+        mask_out[o] = jnp.broadcast_to(by_owner[o:o + 1, :], (8, 128))
+    mask_in[me] = mask_out[me]
+
+    def mask_copy(peer, k):
+        return pltpu.make_async_remote_copy(
+            src_ref=mask_out.at[peer], dst_ref=mask_in.at[me], send_sem=mask_send.at[k],
+            recv_sem=mask_recv.at[me], device_id={"img": peer},
+        )
+
+    for k, peer in enumerate(peers):
+        mask_copy(peer, k).start()
+
+    width = projections.shape[1]
+    for load in loads:
+        load.wait()
+
+    def weigh(t, carry):
+        r = pl.ds(pl.multiple_of(t * 32, 32), 32)
+        total = jnp.zeros((32, 128), jnp.float32)
+        for b in range(width // 128):
+            cols = pl.ds(b * 128, 128)
+            wide = weighted[r, cols].astype(jnp.float32)
+            noise_row = noise[:, cols]
+            total = total + wide * wide * noise_row
+            weighted[r, cols] = (wide * noise_row).astype(jnp.bfloat16)
+        power[r, :] = jnp.broadcast_to(
+            0.5 * jnp.sum(total, axis=1, keepdims=True), (32, 128)
+        )
+        return carry
+
+    lax.fori_loop(0, block_dirs // 32, weigh, 0)
+    own_load.wait()
+
+    def chunk_rows(ch):
+        return pl.ds(pl.multiple_of(ch * pair, pair), pair)
+
+    def store(ch):
+        at = chunk_rows(ch)
+        return pltpu.make_async_copy(held.at[at], gathered_out.at[at], store_sem.at[ch])
+
+    def score(kind):
+        zs, ok = source(kind)
+        ys = y if kind[1] else 1 - y
+
+        def body():
+            for h in range(PIECES):
+                wait_arrival(zs, ys, 1 - c, h)
+            ch = zs * NY + ys
+            store(ch).start()
+            at = chunk_rows(ch)
+
+            def first(t, top):
+                r = pl.ds(pl.multiple_of(t * TILE_ROWS, TILE_ROWS), TILE_ROWS)
+                s = lax.dot_general(
+                    weighted[r, :], held[at, :], (((1,), (1,)), ((), ())),
+                    preferred_element_type=jnp.float32,
+                ) - power[r, :]
+                scores[ch, r, :] = s
+                return jnp.maximum(top, jnp.max(s, axis=0, keepdims=True))
+
+            top = lax.fori_loop(
+                0, block_dirs // TILE_ROWS, first, jnp.full((1, pair), LOW, jnp.float32)
+            )
+
+            def second(t, total):
+                r = pl.ds(pl.multiple_of(t * 256, 256), 256)
+                e = jnp.exp(scores[ch, r, :] - top)
+                scores[ch, r, :] = e
+                return total + jnp.sum(e, axis=0, keepdims=True)
+
+            total = lax.fori_loop(
+                0, block_dirs // 256, second, jnp.zeros((1, pair), jnp.float32)
+            )
+            stats[me, 0, pl.ds(ch, 1), :] = top
+            stats[me, 1, pl.ds(ch, 1), :] = total
+
+        guarded(ok, body)
+
+    L, R = -1, 1
+    ACROSS = (0, False, 0)
+    score(OWN)
+    relay(ACROSS, 1)
+    relay((L, True, 1), 1)
+    relay((R, True, 1), 1)
+    relay(ACROSS, 0)
+    relay((L, True, 1), 0)
+    relay((R, True, 1), 0)
+    score(ACROSS)
+    relay((L, True, 2), 1)
+    relay((R, True, 2), 1)
+    score((L, True, 1))
+    relay((L, True, 2), 0)
+    relay((R, True, 2), 0)
+    score((R, True, 1))
+    for h in (1, 0):
+        for side in (L, R):
+            relay((side, False, 1), h)
+    score((L, True, 2))
+    score((R, True, 2))
+    for h in (1, 0):
+        for side in (L, R):
+            relay((side, True, 3), h)
+    score((L, False, 1))
+    score((R, False, 1))
+    for h in (1, 0):
+        for side in (L, R):
+            relay((side, False, 2), h)
+    score((L, True, 3))
+    score((R, True, 3))
+    score((L, False, 2))
+    score((R, False, 2))
+    for h in (1, 0):
+        for side in (L, R):
+            relay((side, False, 3), h)
+    score((L, False, 3))
+    score((R, False, 3))
+
+    for k, peer in enumerate(peers):
+        pltpu.make_async_remote_copy(
+            src_ref=mask_in.at[peer], dst_ref=mask_in.at[peer], send_sem=mask_send.at[k],
+            recv_sem=mask_recv.at[peer], device_id={"img": me},
+        ).wait_recv()
+    for ch in range(chips):
+        masks[ch:ch + 1, :] = mask_in[ch * NC][0:1, :] + mask_in[ch * NC + 1][0:1, :]
+    is_live = masks[...] > 0.5
+    top = stats[me, 0]
+    stats[me, 0] = jnp.where(is_live, top, LOW)
+    stats[me, 1] = jnp.where(is_live, stats[me, 1], 0.0)
+
+    def stat_copy(peer, k):
+        return pltpu.make_async_remote_copy(
+            src_ref=stats.at[me], dst_ref=stats.at[me], send_sem=stat_send.at[k],
+            recv_sem=stat_recv.at[me], device_id={"img": peer},
+        )
+
+    for k, peer in enumerate(peers):
+        stat_copy(peer, k).start()
+    for k, peer in enumerate(peers):
+        pltpu.make_async_remote_copy(
+            src_ref=stats.at[peer], dst_ref=stats.at[peer], send_sem=stat_send.at[k],
+            recv_sem=stat_recv.at[peer], device_id={"img": me},
+        ).wait_recv()
+
+    peak = stats[0, 0]
+    for o in range(1, n):
+        peak = jnp.maximum(peak, stats[o, 0])
+    total = jnp.zeros_like(peak)
+    for o in range(n):
+        total = total + stats[o, 1] * jnp.exp(stats[o, 0] - peak)
+    inverse = 1.0 / total
+    scale = jnp.where(is_live, jnp.exp(stats[me, 0] - peak) * inverse, 0.0)
+    masks[...] = peak + jnp.log(total)
+    mine = masks[pl.ds(z * NY + y, 1), :]
+    loglik_out[...] = jnp.where(c == 0, mine[:, :rows], mine[:, rows:])
+
+    def post_copy(ch):
+        return pltpu.make_async_copy(
+            post.at[ch], post_out.at[:, pl.ds(ch * pair, pair)], post_sem.at[ch]
+        )
+
+    for ch in range(chips):
+        row = scale[ch:ch + 1, :]
+
+        def weights(t, carry):
+            r = pl.ds(pl.multiple_of(t * 256, 256), 256)
+            p = (scores[ch, r, :] * row).astype(jnp.bfloat16)
+            post[ch, r, :] = p
+            add = p.astype(jnp.float32)
+            power[r, :] = add if ch == 0 else power[r, :] + add
+            return carry
+
+        lax.fori_loop(0, block_dirs // 256, weights, 0)
+        post_copy(ch).start()
+    for t in range(block_dirs // 128):
+        turned = jnp.transpose(power[t * 128:(t + 1) * 128, :])
+        wsum_out[:, t * 128:(t + 1) * 128] = jnp.sum(turned, axis=0, keepdims=True)
+
+    for h in range(PIECES):
+        settle(OWN, h, True)
+        settle(ACROSS, h, False)
+        for d in range(1, NZ):
+            for side in (L, R):
+                for line in (True, False):
+                    settle((side, line, d), h, False)
+    for k, peer in enumerate(peers):
+        mask_copy(peer, k).wait_send()
+        stat_copy(peer, k).wait_send()
+    for ch in range(chips):
+        store(ch).wait()
+        post_copy(ch).wait()
+
+
+def line_shards(images, projections, noise_weight, owners, counts):
+    rows, width = images.shape
+    dirs = projections.shape[0]
+    n = NZ * NY * NC
+    chips = NZ * NY
+    pair = NC * rows
+    hbm = pl.BlockSpec(memory_space=pl.ANY)
+    vmem = pl.BlockSpec(memory_space=pltpu.VMEM)
+    dma = pltpu.SemaphoreType.DMA
+    gathered, post, weight_sum, loglik = pl.pallas_call(
+        gather_and_score,
+        out_shape=(
+            jax.ShapeDtypeStruct((n * rows, width), jnp.bfloat16),
+            jax.ShapeDtypeStruct((dirs, n * rows), jnp.bfloat16),
+            jax.ShapeDtypeStruct((1, dirs), jnp.float32),
+            jax.ShapeDtypeStruct((1, rows), jnp.float32),
+        ),
+        in_specs=[hbm, hbm, vmem, vmem, vmem],
+        out_specs=(hbm, hbm, vmem, vmem),
+        scratch_shapes=[
+            pltpu.VMEM((n * rows, width), jnp.bfloat16),
+            pltpu.VMEM((dirs, width), jnp.bfloat16),
+            pltpu.VMEM((dirs, 128), jnp.float32),
+            pltpu.VMEM((chips, dirs, pair), jnp.float32),
+            pltpu.VMEM((chips, dirs, pair), jnp.bfloat16),
+            pltpu.VMEM((n, 2, chips, pair), jnp.float32),
+            pltpu.VMEM((n, 8, 128), jnp.float32),
+            pltpu.VMEM((n, 8, 128), jnp.float32),
+            pltpu.VMEM((chips, pair), jnp.float32),
+            dma((dirs // 128,)),
+            dma(()),
+            dma((chips, PIECES, 4)),
+            dma((n, PIECES)),
+            dma((chips,)),
+            dma((chips,)),
+            dma((n - 1,)),
+            dma((n,)),
+            dma((n - 1,)),
+            dma((n,)),
+        ],
+        compiler_params=pltpu.CompilerParams(
+            collective_id=0, has_side_effects=True, vmem_limit_bytes=56 * 1024 * 1024
+        ),
+        cost_estimate=pl.CostEstimate(
+            flops=2 * dirs * n * rows * width, bytes_accessed=20_000_000,
+            transcendentals=dirs * n * rows,
+        ),
+        name="gather_and_score",
+    )(images, projections, noise_weight.reshape(1, -1), owners, counts.reshape(-1, 1))
+    backproj = lax.dot_general(
+        post, gathered, (((1,), (0,)), ((), ())), preferred_element_type=jnp.float32
+    ).astype(jnp.bfloat16)
+    return backproj, weight_sum.reshape(-1), loglik.reshape(-1)
 
 
 def slot_layout(owners, devices, capacity):
@@ -79,4 +469,5 @@
         P(("grp", "img")),
     )
     out_specs = (P(("grp", "img"), None), P(("grp", "img")), P(("grp", "img")))
-    return jax.shard_map(shards, mesh=mesh, in_specs=in_specs, out_specs=out_specs, check_vma=False)
+    body = line_shards if mesh.shape["img"] == NZ * NY * NC else shards
+    return jax.shard_map(body, mesh=mesh, in_specs=in_specs, out_specs=out_specs, check_vma=False)

time: 201 us -> 73.4 us (0.37)
  waiting for transfers between devices: 96.8 us -> 0 us
  Pallas kernels: 0 us -> 55 us
  blocking collectives: 35.9 us -> 0 us
  starting transfers between devices: 23.7 us -> 0 us
  other arithmetic: 12.3 us -> 0 us
  local copies, waits for them, and re-layouts: 13.9 us -> 5.18 us
  matrix products: 16.5 us -> 12.3 us
    all_to_all x2 -> x0, waiting for transfers between devices: 96.8 us -> none  [the longest x1 57.1 us: shards(): lax.all_to_all(outgoing.reshape(devices, capacity, width), 'img', split_a...]
    pallas_call x0 -> x1, Pallas kernels: none -> 55 us  [line_shards(): pl.pallas_call(gather_and_score, out_shape=(jax.ShapeDtypeStruct((n * row...]
    all_to_all x1 -> x0, blocking collectives: 35.9 us -> none  [shards(): lax.all_to_all(outgoing_post.reshape(devices, capacity, block_dirs), 'img...]
    all_to_all x2 -> x0, starting transfers between devices: 23.7 us -> none  [the longest x1 16.1 us: shards(): lax.all_to_all(scores.reshape(devices, capacity, block_dirs), 'img', spli...]
    scatter x1 -> x0, local copies, waits for them, and re-layouts: 9.91 us -> none  [shards(): jnp.zeros((devices * capacity, width), jnp.bfloat16).at[target]]
    reduce_sum x5 -> x0, other arithmetic: 6.55 us -> none  [the longest x1 4.62 us: shards(): power = jnp.sum(proj_wide * proj_wide * noise_weight[None, :], axis=1)]
    dot_general x2 -> x1, matrix products: 16.5 us -> 12.3 us  [line_shards(): lax.dot_general(post, gathered, (((1,), (0,)), ((), ())), preferred_eleme...]
    reshape x1 -> x2, local copies, waits for them, and re-layouts: 0.1 us -> 2.68 us  [the longest x1 1.35 us: line_shards(): counts.reshape(-1, 1)]
  transfers between devices with their start and end apart: 2 -> 0, of which waited for: 2 -> 0; matrix products, arithmetic and copies ran while one was open for 3% -> 0% of each run, Pallas kernels for 0% -> 0%
where the time goes in v1:
time: 73.4 us; the launch traced here: 73.1 us
  Pallas kernels  55 us (75%)
  matrix products  12.3 us (17%)
  local copies, waits for them, and re-layouts  5.18 us (7%)
    pallas_call x1, Pallas kernels, line_shards(): pl.pallas_call(gather_and_score, out_shape=(jax.ShapeDtypeStruct((n * row...  55 us
    dot_general x1, matrix products, line_shards(): lax.dot_general(post, gathered, (((1,), (0,)), ((), ())), preferred_eleme...  12.3 us
    unnamed x7, local copies, waits for them, and re-layouts  2.5 us

profile of v1, /device:TPU:0, one launch (start us, length us, event | category | flops | bytes accessed | tf_op | source)
XLA Modules:
  0.0 73.1 jit_solution(6948620097269414114)
XLA Ops:
  0.6 1.3 %reshape.18.noise = f32[1,3200]{1,0:T(1,128)} reshape(f32[3200]{0:T(1024)} %param.7) | data formatting | bytes 25600 | tf_op jit(solution)/shard_map/reshape | solution.py:390
  2.0 1.4 %copy.8.owners = s32[64,4]{1,0:T(8,128)} copy(s32[64,4]{0,1:T(4,128)} %param.8) | data formatting | bytes 2048 | tf_op args[3]
  3.3 1.4 %copy.9.counts = s32[64,1]{1,0:T(8,128)} copy(s32[64,1]{0,1:T(1,128)} %bitcast.6) | data formatting | bytes 512 | tf_op jit(solution)/shard_map/reshape | solution.py:390
  4.7 55.0 %gather_and_score.1 = (bf16[1024,3200]{1,0:T(8,128)(2,1)}, bf16[1024,1024]{1,0:T(8,128)(2,1)}, f32[1,1024]{1,0:T(1,128)}, f32[1,64]{1,0:T(1,128)}) custom-call(bf16[64,3200]{1,0:T(8,128)(2,1)} %images.1, bf16[1024,3200]{1,0:T(8,128)(2,1)} %projections.1, f32[1,3200]{1,0:T(1,128)} %reshape.18.noise, s32[64,4]{1,0:T(8,128)} %copy.8.owners, s32[64,1]{1,0:T(8,128)} %copy.9.counts), custom_call_target="tpu_custom_call" | custom-call | flops 6710886400 | bytes 20000000 | tf_op jit(solution)/shard_map/gather_and_score/pallas_call | solution.py:351
  59.7 0.0 copy-start
  59.7 0.0 copy-start.1
  59.7 12.3 %convolution_convert_fusion = bf16[1024,3200]{1,0:T(8,128)(2,1)} fusion(bf16[1024,1024]{1,0:T(8,128)(2,1)} %get-tuple-element.7, bf16[1024,3200]{1,0:T(8,128)(2,1)} %get-tuple-element.8), kind=kOutput, calls=%fused_computation | convolution fusion | flops 6714163200 | bytes 15204352 | tf_op jit(solution)/shard_map/dot_general | solution.py:391
  72.0 0.0 copy-done
  72.0 0.6 copy.12
  72.6 0.0 copy-done.1
  72.6 0.5 copy.13
Async XLA Ops:
  59.7 12.3 %copy-start = (f32[1,1024]{1,0:T(1,128)S(1)}, f32[1,1024]{1,0:T(1,128)}, u32[]{:S(2)}) copy-start(f32[1,1024]{1,0:T(1,128)} %get-tuple-element.9) | copy-start | bytes 12292
  59.7 12.9 %copy-start.1 = (f32[1,64]{1,0:T(1,128)S(1)}, f32[1,64]{1,0:T(1,128)}, u32[]{:S(2)}) copy-start(f32[1,64]{1,0:T(1,128)} %get-tuple-element.10) | copy-start | bytes 772

commit v2 on v1

--- a/solution.py
+++ b/solution.py
@@ -13,8 +13,8 @@
 
 def gather_and_score(
     images, projections, noise, owners, counts,
-    gathered_out, post_out, wsum_out, loglik_out,
-    held, weighted, power, scores, post, stats, mask_out, mask_in, masks,
+    gathered_out, post_out, loglik_out,
+    held, weighted, power, scores, post, local, stats, mask_out, mask_in, masks, lse,
     load_sem, own_sem, send_sem, recv_sem, store_sem, post_sem,
     mask_send, mask_recv, stat_send, stat_recv,
 ):
@@ -131,20 +131,19 @@
 
         guarded(ok, body)
 
+    local[...] = jnp.zeros_like(local)
     OWN = (0, True, 0)
     for h in (1, 0):
         act(copies(z, True, h, True, (1, -1)), lambda copy: copy.start())
 
-    lane = lax.broadcasted_iota(jnp.int32, (rows, 128), 1)
-    count = counts[...]
-    live = jnp.zeros((rows, 128), jnp.bool_)
-    for k in range(owners.shape[1]):
-        live = live | ((lane == owners[:, k:k + 1]) & (count > k))
-    spot = lax.broadcasted_iota(jnp.int32, (rows, 128), 0) + c * rows
-    pick = jnp.where(lane == spot, 1.0, 0.0)
-    by_owner = lax.dot_general(
-        jnp.where(live, 1.0, 0.0).astype(jnp.bfloat16), pick.astype(jnp.bfloat16),
-        (((0,), (0,)), ((), ())), preferred_element_type=jnp.float32,
+    owner = lax.broadcasted_iota(jnp.int32, (n, rows), 0)
+    count = counts[...].reshape(1, rows)
+    live = jnp.zeros((n, rows), jnp.float32)
+    for k in range(owners.shape[0]):
+        live = live + jnp.where((owners[k:k + 1, :] == owner) & (count > k), 1.0, 0.0)
+    none = jnp.zeros_like(live)
+    by_owner = jnp.concatenate(
+        [jnp.where(c == 0, live, none), jnp.where(c == 0, none, live)], axis=1
     )
     for o in range(n):
         mask_out[o] = jnp.broadcast_to(by_owner[o:o + 1, :], (8, 128))
@@ -169,7 +168,7 @@
         for b in range(width // 128):
             cols = pl.ds(b * 128, 128)
             wide = weighted[r, cols].astype(jnp.float32)
-            noise_row = noise[:, cols]
+            noise_row = noise[cols].reshape(1, 128)
             total = total + wide * wide * noise_row
             weighted[r, cols] = (wide * noise_row).astype(jnp.bfloat16)
         power[r, :] = jnp.broadcast_to(
@@ -220,17 +219,74 @@
             total = lax.fori_loop(
                 0, block_dirs // 256, second, jnp.zeros((1, pair), jnp.float32)
             )
-            stats[me, 0, pl.ds(ch, 1), :] = top
-            stats[me, 1, pl.ds(ch, 1), :] = total
+            local[0, pl.ds(ch, 1), :] = top
+            local[1, pl.ds(ch, 1), :] = total
 
         guarded(ok, body)
+
+    def offer(phase):
+        if phase == 0:
+            for k, peer in enumerate(peers):
+                pltpu.make_async_remote_copy(
+                    src_ref=mask_in.at[peer], dst_ref=mask_in.at[peer],
+                    send_sem=mask_send.at[k], recv_sem=mask_recv.at[peer],
+                    device_id={"img": me},
+                ).wait_recv()
+            for ch in range(chips):
+                masks[ch:ch + 1, :] = mask_in[ch * NC][0:1, :] + mask_in[ch * NC + 1][0:1, :]
+        is_live = masks[...] > 0.5
+        stats[phase, me, 0] = jnp.where(is_live, local[0], LOW)
+        stats[phase, me, 1] = jnp.where(is_live, local[1], 0.0)
+        for k, peer in enumerate(peers):
+            stat_copy(phase, peer, k).start()
+
+    def stat_copy(phase, peer, k):
+        return pltpu.make_async_remote_copy(
+            src_ref=stats.at[phase, me], dst_ref=stats.at[phase, me],
+            send_sem=stat_send.at[phase, k], recv_sem=stat_recv.at[phase, me],
+            device_id={"img": peer},
+        )
+
+    def post_copy(ch):
+        return pltpu.make_async_copy(
+            post.at[ch], post_out.at[:, pl.ds(ch * pair, pair)], post_sem.at[ch]
+        )
+
+    def conclude(phase, chunks):
+        for k, peer in enumerate(peers):
+            pltpu.make_async_remote_copy(
+                src_ref=stats.at[phase, peer], dst_ref=stats.at[phase, peer],
+                send_sem=stat_send.at[phase, k], recv_sem=stat_recv.at[phase, peer],
+                device_id={"img": me},
+            ).wait_recv()
+        peak = stats[phase, 0, 0]
+        for o in range(1, n):
+            peak = jnp.maximum(peak, stats[phase, o, 0])
+        total = jnp.zeros_like(peak)
+        for o in range(n):
+            total = total + stats[phase, o, 1] * jnp.exp(stats[phase, o, 0] - peak)
+        inverse = 1.0 / total
+        scale = jnp.where(masks[...] > 0.5, jnp.exp(stats[phase, me, 0] - peak) * inverse, 0.0)
+        logs = peak + jnp.log(total)
+        for ch in chunks:
+            lse[ch:ch + 1, :] = logs[ch:ch + 1, :]
+        for ch in chunks:
+            row = scale[ch:ch + 1, :]
+
+            def weights(t, carry):
+                r = pl.ds(pl.multiple_of(t * 256, 256), 256)
+                post[ch, r, :] = (scores[ch, r, :] * row).astype(jnp.bfloat16)
+                return carry
+
+            lax.fori_loop(0, block_dirs // 256, weights, 0)
+            post_copy(ch).start()
 
     L, R = -1, 1
     ACROSS = (0, False, 0)
-    score(OWN)
     relay(ACROSS, 1)
     relay((L, True, 1), 1)
     relay((R, True, 1), 1)
+    score(OWN)
     relay(ACROSS, 0)
     relay((L, True, 1), 0)
     relay((R, True, 1), 0)
@@ -254,89 +310,88 @@
     for h in (1, 0):
         for side in (L, R):
             relay((side, False, 2), h)
+    score((L, False, 2))
+    score((R, False, 2))
+    inner = [ch for ch in range(chips) if 0 < ch // NY < NZ - 1]
+    outer = [ch for ch in range(chips) if ch not in inner]
+    offer(0)
     score((L, True, 3))
     score((R, True, 3))
-    score((L, False, 2))
-    score((R, False, 2))
-    for h in (1, 0):
-        for side in (L, R):
-            relay((side, False, 3), h)
-    score((L, False, 3))
-    score((R, False, 3))
-
-    for k, peer in enumerate(peers):
-        pltpu.make_async_remote_copy(
-            src_ref=mask_in.at[peer], dst_ref=mask_in.at[peer], send_sem=mask_send.at[k],
-            recv_sem=mask_recv.at[peer], device_id={"img": me},
-        ).wait_recv()
-    for ch in range(chips):
-        masks[ch:ch + 1, :] = mask_in[ch * NC][0:1, :] + mask_in[ch * NC + 1][0:1, :]
-    is_live = masks[...] > 0.5
-    top = stats[me, 0]
-    stats[me, 0] = jnp.where(is_live, top, LOW)
-    stats[me, 1] = jnp.where(is_live, stats[me, 1], 0.0)
-
-    def stat_copy(peer, k):
-        return pltpu.make_async_remote_copy(
-            src_ref=stats.at[me], dst_ref=stats.at[me], send_sem=stat_send.at[k],
-            recv_sem=stat_recv.at[me], device_id={"img": peer},
-        )
-
-    for k, peer in enumerate(peers):
-        stat_copy(peer, k).start()
-    for k, peer in enumerate(peers):
-        pltpu.make_async_remote_copy(
-            src_ref=stats.at[peer], dst_ref=stats.at[peer], send_sem=stat_send.at[k],
-            recv_sem=stat_recv.at[peer], device_id={"img": me},
-        ).wait_recv()
-
-    peak = stats[0, 0]
-    for o in range(1, n):
-        peak = jnp.maximum(peak, stats[o, 0])
-    total = jnp.zeros_like(peak)
-    for o in range(n):
-        total = total + stats[o, 1] * jnp.exp(stats[o, 0] - peak)
-    inverse = 1.0 / total
-    scale = jnp.where(is_live, jnp.exp(stats[me, 0] - peak) * inverse, 0.0)
-    masks[...] = peak + jnp.log(total)
-    mine = masks[pl.ds(z * NY + y, 1), :]
-    loglik_out[...] = jnp.where(c == 0, mine[:, :rows], mine[:, rows:])
-
-    def post_copy(ch):
-        return pltpu.make_async_copy(
-            post.at[ch], post_out.at[:, pl.ds(ch * pair, pair)], post_sem.at[ch]
-        )
-
-    for ch in range(chips):
-        row = scale[ch:ch + 1, :]
-
-        def weights(t, carry):
-            r = pl.ds(pl.multiple_of(t * 256, 256), 256)
-            p = (scores[ch, r, :] * row).astype(jnp.bfloat16)
-            post[ch, r, :] = p
-            add = p.astype(jnp.float32)
-            power[r, :] = add if ch == 0 else power[r, :] + add
-            return carry
-
-        lax.fori_loop(0, block_dirs // 256, weights, 0)
-        post_copy(ch).start()
-    for t in range(block_dirs // 128):
-        turned = jnp.transpose(power[t * 128:(t + 1) * 128, :])
-        wsum_out[:, t * 128:(t + 1) * 128] = jnp.sum(turned, axis=0, keepdims=True)
-
     for h in range(PIECES):
         settle(OWN, h, True)
         settle(ACROSS, h, False)
-        for d in range(1, NZ):
-            for side in (L, R):
-                for line in (True, False):
-                    settle((side, line, d), h, False)
+        for side in (L, R):
+            for line in (True, False):
+                settle((side, line, 1), h, False)
+    conclude(0, inner)
+    for h in (1, 0):
+        for side in (L, R):
+            relay((side, False, 3), h)
+    for h in range(PIECES):
+        for side in (L, R):
+            settle((side, True, 2), h, False)
+            settle((side, False, 2), h, False)
+    score((L, False, 3))
+    score((R, False, 3))
+    offer(1)
+    for h in range(PIECES):
+        for side in (L, R):
+            settle((side, True, 3), h, False)
+            settle((side, False, 3), h, False)
     for k, peer in enumerate(peers):
         mask_copy(peer, k).wait_send()
-        stat_copy(peer, k).wait_send()
+        stat_copy(0, peer, k).wait_send()
     for ch in range(chips):
         store(ch).wait()
+    conclude(1, outer)
+    mine = lse[pl.ds(z * NY + y, 1), :]
+    loglik_out[...] = jnp.where(c == 0, mine[:, :rows], mine[:, rows:]).reshape(rows)
+    for k, peer in enumerate(peers):
+        stat_copy(1, peer, k).wait_send()
+    for ch in range(chips):
         post_copy(ch).wait()
+
+
+BACK_COLS = 512
+
+
+def back(post, gathered, loglik, out, wsum_out, loglik_out, weights, held, total, sems, out_sems):
+    dirs, depth = weights.shape
+    width = held.shape[1]
+    spans = [(b, min(BACK_COLS, width - b)) for b in range(0, width, BACK_COLS)]
+    first = pltpu.make_async_copy(post, weights, sems.at[len(spans)])
+    first.start()
+    loads, saves = [], []
+    for j, (b, size) in enumerate(spans):
+        cols = pl.ds(b, size)
+        loads.append(pltpu.make_async_copy(gathered.at[:, cols], held.at[:, cols], sems.at[j]))
+        saves.append(pltpu.make_async_copy(total.at[:, cols], out.at[:, cols], out_sems.at[j]))
+    for load in loads:
+        load.start()
+    loglik_out[...] = loglik[...]
+    first.wait()
+    for j, (b, size) in enumerate(spans):
+        loads[j].wait()
+
+        def tile(t, carry):
+            r = pl.ds(pl.multiple_of(t * 256, 256), 256)
+            total[r, b:b + size] = jnp.dot(
+                weights[r, :], held[:, b:b + size], preferred_element_type=jnp.float32
+            ).astype(jnp.bfloat16)
+            return carry
+
+        lax.fori_loop(0, dirs // 256, tile, 0)
+        saves[j].start()
+        if j == 0:
+            for t in range(dirs // 128):
+                part = jnp.zeros((128, 128), jnp.float32)
+                for k in range(depth // 128):
+                    part = part + weights[t * 128:(t + 1) * 128, k * 128:(k + 1) * 128].astype(
+                        jnp.float32
+                    )
+                wsum_out[t * 128:(t + 1) * 128] = jnp.sum(jnp.transpose(part), axis=0)
+    for save in saves:
+        save.wait()
 
 
 def line_shards(images, projections, noise_weight, owners, counts):
@@ -348,25 +403,26 @@
     hbm = pl.BlockSpec(memory_space=pl.ANY)
     vmem = pl.BlockSpec(memory_space=pltpu.VMEM)
     dma = pltpu.SemaphoreType.DMA
-    gathered, post, weight_sum, loglik = pl.pallas_call(
+    gathered, post, loglik = pl.pallas_call(
         gather_and_score,
         out_shape=(
             jax.ShapeDtypeStruct((n * rows, width), jnp.bfloat16),
             jax.ShapeDtypeStruct((dirs, n * rows), jnp.bfloat16),
-            jax.ShapeDtypeStruct((1, dirs), jnp.float32),
-            jax.ShapeDtypeStruct((1, rows), jnp.float32),
+            jax.ShapeDtypeStruct((rows,), jnp.float32),
         ),
         in_specs=[hbm, hbm, vmem, vmem, vmem],
-        out_specs=(hbm, hbm, vmem, vmem),
+        out_specs=(hbm, hbm, vmem),
         scratch_shapes=[
             pltpu.VMEM((n * rows, width), jnp.bfloat16),
             pltpu.VMEM((dirs, width), jnp.bfloat16),
             pltpu.VMEM((dirs, 128), jnp.float32),
             pltpu.VMEM((chips, dirs, pair), jnp.float32),
             pltpu.VMEM((chips, dirs, pair), jnp.bfloat16),
-            pltpu.VMEM((n, 2, chips, pair), jnp.float32),
+            pltpu.VMEM((2, chips, pair), jnp.float32),
+            pltpu.VMEM((2, n, 2, chips, pair), jnp.float32),
             pltpu.VMEM((n, 8, 128), jnp.float32),
             pltpu.VMEM((n, 8, 128), jnp.float32),
+            pltpu.VMEM((chips, pair), jnp.float32),
             pltpu.VMEM((chips, pair), jnp.float32),
             dma((dirs // 128,)),
             dma(()),
@@ -376,8 +432,8 @@
             dma((chips,)),
             dma((n - 1,)),
             dma((n,)),
-            dma((n - 1,)),
-            dma((n,)),
+            dma((2, n - 1)),
+            dma((2, n)),
         ],
         compiler_params=pltpu.CompilerParams(
             collective_id=0, has_side_effects=True, vmem_limit_bytes=56 * 1024 * 1024
@@ -387,11 +443,30 @@
             transcendentals=dirs * n * rows,
         ),
         name="gather_and_score",
-    )(images, projections, noise_weight.reshape(1, -1), owners, counts.reshape(-1, 1))
-    backproj = lax.dot_general(
-        post, gathered, (((1,), (0,)), ((), ())), preferred_element_type=jnp.float32
-    ).astype(jnp.bfloat16)
-    return backproj, weight_sum.reshape(-1), loglik.reshape(-1)
+    )(images, projections, noise_weight, owners.T, counts)
+    spans = -(-width // BACK_COLS)
+    return pl.pallas_call(
+        back,
+        out_shape=(
+            jax.ShapeDtypeStruct((dirs, width), jnp.bfloat16),
+            jax.ShapeDtypeStruct((dirs,), jnp.float32),
+            jax.ShapeDtypeStruct((rows,), jnp.float32),
+        ),
+        in_specs=[hbm, hbm, vmem],
+        out_specs=(hbm, vmem, vmem),
+        scratch_shapes=[
+            pltpu.VMEM((dirs, n * rows), jnp.bfloat16),
+            pltpu.VMEM((n * rows, width), jnp.bfloat16),
+            pltpu.VMEM((dirs, width), jnp.bfloat16),
+            dma((spans + 1,)),
+            dma((spans,)),
+        ],
+        compiler_params=pltpu.CompilerParams(vmem_limit_bytes=56 * 1024 * 1024),
+        cost_estimate=pl.CostEstimate(
+            flops=2 * dirs * n * rows * width, bytes_accessed=16_000_000, transcendentals=0
+        ),
+        name="back",
+    )(post, gathered, loglik)
 
 
 def slot_layout(owners, devices, capacity):

time: 73.4 us -> 75.9 us (1.034)
  Pallas kernels: 55 us -> 74.9 us
  matrix products: 12.3 us -> 0 us
  local copies, waits for them, and re-layouts: 5.18 us -> 0 us
    pallas_call x0 -> x1, Pallas kernels: none -> 15.9 us  [line_shards(): pl.pallas_call(back, out_shape=(jax.ShapeDtypeStruct((dirs, width), jnp.b...]
    dot_general x1 -> x0, matrix products: 12.3 us -> none  [line_shards(): lax.dot_general(post, gathered, (((1,), (0,)), ((), ())), preferred_eleme...]
    pallas_call x1, Pallas kernels: 55 us -> 59.1 us  [line_shards(): pl.pallas_call(gather_and_score, out_shape=(jax.ShapeDtypeStruct((n * row...]
    reshape x2 -> x0, local copies, waits for them, and re-layouts: 2.68 us -> none  [the longest x1 1.35 us: line_shards(): counts.reshape(-1, 1)]
    unnamed x7 -> x0, local copies, waits for them, and re-layouts: 2.5 us -> none
where the time goes in v2:
time: 75.9 us; the launch traced here: 75.7 us
  Pallas kernels  74.9 us (99%)
  between operations  0.8 us (1%)
    pallas_call x1, Pallas kernels, line_shards(): pl.pallas_call(gather_and_score, out_shape=(jax.ShapeDtypeStruct((n * row...  59.1 us
    pallas_call x1, Pallas kernels, line_shards(): pl.pallas_call(back, out_shape=(jax.ShapeDtypeStruct((dirs, width), jnp.b...  15.9 us

profile of v2, /device:TPU:0, one launch (start us, length us, event | category | flops | bytes accessed | tf_op | source)
XLA Modules:
  0.0 75.7 jit_solution(9964438112015361747)
XLA Ops:
  0.6 59.1 %gather_and_score.1 = (bf16[1024,3200]{1,0:T(8,128)(2,1)}, bf16[1024,1024]{1,0:T(8,128)(2,1)}, f32[64]{0:T(128)}) custom-call(bf16[64,3200]{1,0:T(8,128)(2,1)} %images.1, bf16[1024,3200]{1,0:T(8,128)(2,1)} %projections.1, f32[3200]{0:T(1024)} %noise.1, s32[4,64]{1,0:T(4,128)} %bitcast.1, s32[64]{0:T(128)} %counts.1), custom_call_target="tpu_custom_call" | custom-call | flops 6710886400 | bytes 20000000 | tf_op jit(solution)/shard_map/gather_and_score/pallas_call | solution.py:406
  59.7 15.9 %back.1 = (bf16[1024,3200]{1,0:T(8,128)(2,1)}, f32[1024]{0:T(1024)}, f32[64]{0:T(128)}) custom-call(bf16[1024,1024]{1,0:T(8,128)(2,1)} %get-tuple-element.6.post, bf16[1024,3200]{1,0:T(8,128)(2,1)} %get-tuple-element.7.gathered, f32[64]{0:T(128)} %get-tuple-element.8.loglik), custom_call_target="tpu_custom_call" | custom-call | flops 6710886400 | bytes 16000000 | tf_op jit(solution)/shard_map/back/pallas_call | solution.py:448

commit v3 on v2

--- a/solution.py
+++ b/solution.py
@@ -8,7 +8,7 @@
 NZ, NY, NC = 4, 2, 2
 PIECES = 2
 LOW = -1e30
-TILE_ROWS = 512
+TILE_ROWS = 1024
 
 
 def gather_and_score(
@@ -224,26 +224,25 @@
 
         guarded(ok, body)
 
-    def offer(phase):
-        if phase == 0:
-            for k, peer in enumerate(peers):
-                pltpu.make_async_remote_copy(
-                    src_ref=mask_in.at[peer], dst_ref=mask_in.at[peer],
-                    send_sem=mask_send.at[k], recv_sem=mask_recv.at[peer],
-                    device_id={"img": me},
-                ).wait_recv()
-            for ch in range(chips):
-                masks[ch:ch + 1, :] = mask_in[ch * NC][0:1, :] + mask_in[ch * NC + 1][0:1, :]
+    def offer():
+        for k, peer in enumerate(peers):
+            pltpu.make_async_remote_copy(
+                src_ref=mask_in.at[peer], dst_ref=mask_in.at[peer],
+                send_sem=mask_send.at[k], recv_sem=mask_recv.at[peer],
+                device_id={"img": me},
+            ).wait_recv()
+        for ch in range(chips):
+            masks[ch:ch + 1, :] = mask_in[ch * NC][0:1, :] + mask_in[ch * NC + 1][0:1, :]
         is_live = masks[...] > 0.5
-        stats[phase, me, 0] = jnp.where(is_live, local[0], LOW)
-        stats[phase, me, 1] = jnp.where(is_live, local[1], 0.0)
+        stats[me, 0] = jnp.where(is_live, local[0], LOW)
+        stats[me, 1] = jnp.where(is_live, local[1], 0.0)
         for k, peer in enumerate(peers):
-            stat_copy(phase, peer, k).start()
-
-    def stat_copy(phase, peer, k):
+            stat_copy(peer, k).start()
+
+    def stat_copy(peer, k):
         return pltpu.make_async_remote_copy(
-            src_ref=stats.at[phase, me], dst_ref=stats.at[phase, me],
-            send_sem=stat_send.at[phase, k], recv_sem=stat_recv.at[phase, me],
+            src_ref=stats.at[me], dst_ref=stats.at[me],
+            send_sem=stat_send.at[k], recv_sem=stat_recv.at[me],
             device_id={"img": peer},
         )
 
@@ -252,21 +251,21 @@
             post.at[ch], post_out.at[:, pl.ds(ch * pair, pair)], post_sem.at[ch]
         )
 
-    def conclude(phase, chunks):
+    def conclude(chunks):
         for k, peer in enumerate(peers):
             pltpu.make_async_remote_copy(
-                src_ref=stats.at[phase, peer], dst_ref=stats.at[phase, peer],
-                send_sem=stat_send.at[phase, k], recv_sem=stat_recv.at[phase, peer],
+                src_ref=stats.at[peer], dst_ref=stats.at[peer],
+                send_sem=stat_send.at[k], recv_sem=stat_recv.at[peer],
                 device_id={"img": me},
             ).wait_recv()
-        peak = stats[phase, 0, 0]
+        peak = stats[0, 0]
         for o in range(1, n):
-            peak = jnp.maximum(peak, stats[phase, o, 0])
+            peak = jnp.maximum(peak, stats[o, 0])
         total = jnp.zeros_like(peak)
         for o in range(n):
-            total = total + stats[phase, o, 1] * jnp.exp(stats[phase, o, 0] - peak)
+            total = total + stats[o, 1] * jnp.exp(stats[o, 0] - peak)
         inverse = 1.0 / total
-        scale = jnp.where(masks[...] > 0.5, jnp.exp(stats[phase, me, 0] - peak) * inverse, 0.0)
+        scale = jnp.where(masks[...] > 0.5, jnp.exp(stats[me, 0] - peak) * inverse, 0.0)
         logs = peak + jnp.log(total)
         for ch in chunks:
             lse[ch:ch + 1, :] = logs[ch:ch + 1, :]
@@ -312,47 +311,39 @@
             relay((side, False, 2), h)
     score((L, False, 2))
     score((R, False, 2))
-    inner = [ch for ch in range(chips) if 0 < ch // NY < NZ - 1]
-    outer = [ch for ch in range(chips) if ch not in inner]
-    offer(0)
     score((L, True, 3))
     score((R, True, 3))
-    for h in range(PIECES):
-        settle(OWN, h, True)
-        settle(ACROSS, h, False)
-        for side in (L, R):
-            for line in (True, False):
-                settle((side, line, 1), h, False)
-    conclude(0, inner)
     for h in (1, 0):
         for side in (L, R):
             relay((side, False, 3), h)
     for h in range(PIECES):
-        for side in (L, R):
-            settle((side, True, 2), h, False)
-            settle((side, False, 2), h, False)
+        settle(OWN, h, True)
+        settle(ACROSS, h, False)
+        for d in (1, 2):
+            for side in (L, R):
+                for line in (True, False):
+                    settle((side, line, d), h, False)
     score((L, False, 3))
     score((R, False, 3))
-    offer(1)
+    offer()
     for h in range(PIECES):
         for side in (L, R):
             settle((side, True, 3), h, False)
             settle((side, False, 3), h, False)
     for k, peer in enumerate(peers):
         mask_copy(peer, k).wait_send()
-        stat_copy(0, peer, k).wait_send()
     for ch in range(chips):
         store(ch).wait()
-    conclude(1, outer)
+    conclude(range(chips))
     mine = lse[pl.ds(z * NY + y, 1), :]
     loglik_out[...] = jnp.where(c == 0, mine[:, :rows], mine[:, rows:]).reshape(rows)
     for k, peer in enumerate(peers):
-        stat_copy(1, peer, k).wait_send()
+        stat_copy(peer, k).wait_send()
     for ch in range(chips):
         post_copy(ch).wait()
 
 
-BACK_COLS = 512
+BACK_ROWS, BACK_COLS = 512, 512
 
 
 def back(post, gathered, loglik, out, wsum_out, loglik_out, weights, held, total, sems, out_sems):
@@ -373,23 +364,17 @@
     for j, (b, size) in enumerate(spans):
         loads[j].wait()
 
-        def tile(t, carry):
-            r = pl.ds(pl.multiple_of(t * 256, 256), 256)
-            total[r, b:b + size] = jnp.dot(
-                weights[r, :], held[:, b:b + size], preferred_element_type=jnp.float32
+        for t in range(0, dirs, BACK_ROWS):
+            total[t:t + BACK_ROWS, b:b + size] = jnp.dot(
+                weights[t:t + BACK_ROWS, :], held[:, b:b + size],
+                preferred_element_type=jnp.float32,
             ).astype(jnp.bfloat16)
-            return carry
-
-        lax.fori_loop(0, dirs // 256, tile, 0)
         saves[j].start()
-        if j == 0:
-            for t in range(dirs // 128):
-                part = jnp.zeros((128, 128), jnp.float32)
-                for k in range(depth // 128):
-                    part = part + weights[t * 128:(t + 1) * 128, k * 128:(k + 1) * 128].astype(
-                        jnp.float32
-                    )
-                wsum_out[t * 128:(t + 1) * 128] = jnp.sum(jnp.transpose(part), axis=0)
+    for t in range(dirs // 128):
+        part = jnp.zeros((128, 128), jnp.float32)
+        for k in range(depth // 128):
+            part = part + weights[t * 128:(t + 1) * 128, k * 128:(k + 1) * 128].astype(jnp.float32)
+        wsum_out[t * 128:(t + 1) * 128] = jnp.sum(jnp.transpose(part), axis=0)
     for save in saves:
         save.wait()
 
@@ -419,7 +404,7 @@
             pltpu.VMEM((chips, dirs, pair), jnp.float32),
             pltpu.VMEM((chips, dirs, pair), jnp.bfloat16),
             pltpu.VMEM((2, chips, pair), jnp.float32),
-            pltpu.VMEM((2, n, 2, chips, pair), jnp.float32),
+            pltpu.VMEM((n, 2, chips, pair), jnp.float32),
             pltpu.VMEM((n, 8, 128), jnp.float32),
             pltpu.VMEM((n, 8, 128), jnp.float32),
             pltpu.VMEM((chips, pair), jnp.float32),
@@ -432,8 +417,8 @@
             dma((chips,)),
             dma((n - 1,)),
             dma((n,)),
-            dma((2, n - 1)),
-            dma((2, n)),
+            dma((n - 1,)),
+            dma((n,)),
         ],
         compiler_params=pltpu.CompilerParams(
             collective_id=0, has_side_effects=True, vmem_limit_bytes=56 * 1024 * 1024

time: 75.9 us -> 67.3 us (0.89)
  Pallas kernels: 74.9 us -> 66.4 us
    pallas_call x1, Pallas kernels: 59.1 us -> 54.2 us  [line_shards(): pl.pallas_call(gather_and_score, out_shape=(jax.ShapeDtypeStruct((n * row...]
    pallas_call x1, Pallas kernels: 15.9 us -> 12.2 us  [line_shards(): pl.pallas_call(back, out_shape=(jax.ShapeDtypeStruct((dirs, width), jnp.b...]
where the time goes in v3:
time: 67.3 us; the launch traced here: 67.2 us
  Pallas kernels  66.4 us (99%)
  between operations  0.8 us (1%)
    pallas_call x1, Pallas kernels, line_shards(): pl.pallas_call(gather_and_score, out_shape=(jax.ShapeDtypeStruct((n * row...  54.2 us
    pallas_call x1, Pallas kernels, line_shards(): pl.pallas_call(back, out_shape=(jax.ShapeDtypeStruct((dirs, width), jnp.b...  12.2 us

profile of v3, /device:TPU:0, one launch (start us, length us, event | category | flops | bytes accessed | tf_op | source)
XLA Modules:
  0.0 67.2 jit_solution(13219102940848477897)
XLA Ops:
  0.6 54.2 %gather_and_score.1 = (bf16[1024,3200]{1,0:T(8,128)(2,1)}, bf16[1024,1024]{1,0:T(8,128)(2,1)}, f32[64]{0:T(128)}) custom-call(bf16[64,3200]{1,0:T(8,128)(2,1)} %images.1, bf16[1024,3200]{1,0:T(8,128)(2,1)} %projections.1, f32[3200]{0:T(1024)} %noise.1, s32[4,64]{1,0:T(4,128)} %bitcast.1, s32[64]{0:T(128)} %counts.1), custom_call_target="tpu_custom_call" | custom-call | flops 6710886400 | bytes 20000000 | tf_op jit(solution)/shard_map/gather_and_score/pallas_call | solution.py:391
  54.8 12.2 %back.1 = (bf16[1024,3200]{1,0:T(8,128)(2,1)}, f32[1024]{0:T(1024)}, f32[64]{0:T(128)}) custom-call(bf16[1024,1024]{1,0:T(8,128)(2,1)} %get-tuple-element.6.post, bf16[1024,3200]{1,0:T(8,128)(2,1)} %get-tuple-element.7.gathered, f32[64]{0:T(128)} %get-tuple-element.8.loglik), custom_call_target="tpu_custom_call" | custom-call | flops 6710886400 | bytes 16000000 | tf_op jit(solution)/shard_map/back/pallas_call | solution.py:433

commit v4 on v3

--- a/solution.py
+++ b/solution.py
@@ -301,11 +301,11 @@
             relay((side, False, 1), h)
     score((L, True, 2))
     score((R, True, 2))
+    score((L, False, 1))
+    score((R, False, 1))
     for h in (1, 0):
         for side in (L, R):
             relay((side, True, 3), h)
-    score((L, False, 1))
-    score((R, False, 1))
     for h in (1, 0):
         for side in (L, R):
             relay((side, False, 2), h)
@@ -313,9 +313,6 @@
     score((R, False, 2))
     score((L, True, 3))
     score((R, True, 3))
-    for h in (1, 0):
-        for side in (L, R):
-            relay((side, False, 3), h)
     for h in range(PIECES):
         settle(OWN, h, True)
         settle(ACROSS, h, False)
@@ -323,6 +320,9 @@
             for side in (L, R):
                 for line in (True, False):
                     settle((side, line, d), h, False)
+    for h in (1, 0):
+        for side in (L, R):
+            relay((side, False, 3), h)
     score((L, False, 3))
     score((R, False, 3))
     offer()

time: 67.3 us -> 66.9 us (level)
  no operation moved by 1% of the time
where the time goes in v4:
time: 66.9 us; the launch traced here: 66.8 us
  Pallas kernels  66 us (99%)
  between operations  0.8 us (1%)
    pallas_call x1, Pallas kernels, line_shards(): pl.pallas_call(gather_and_score, out_shape=(jax.ShapeDtypeStruct((n * row...  53.8 us
    pallas_call x1, Pallas kernels, line_shards(): pl.pallas_call(back, out_shape=(jax.ShapeDtypeStruct((dirs, width), jnp.b...  12.2 us

profile of v4, /device:TPU:0, one launch (start us, length us, event | category | flops | bytes accessed | tf_op | source)
XLA Modules:
  0.0 66.8 jit_solution(17230570685566442329)
XLA Ops:
  0.6 53.8 %gather_and_score.1 = (bf16[1024,3200]{1,0:T(8,128)(2,1)}, bf16[1024,1024]{1,0:T(8,128)(2,1)}, f32[64]{0:T(128)}) custom-call(bf16[64,3200]{1,0:T(8,128)(2,1)} %images.1, bf16[1024,3200]{1,0:T(8,128)(2,1)} %projections.1, f32[3200]{0:T(1024)} %noise.1, s32[4,64]{1,0:T(4,128)} %bitcast.1, s32[64]{0:T(128)} %counts.1), custom_call_target="tpu_custom_call" | custom-call | flops 6710886400 | bytes 20000000 | tf_op jit(solution)/shard_map/gather_and_score/pallas_call | solution.py:391
  54.4 12.2 %back.1 = (bf16[1024,3200]{1,0:T(8,128)(2,1)}, f32[1024]{0:T(1024)}, f32[64]{0:T(128)}) custom-call(bf16[1024,1024]{1,0:T(8,128)(2,1)} %get-tuple-element.6.post, bf16[1024,3200]{1,0:T(8,128)(2,1)} %get-tuple-element.7.gathered, f32[64]{0:T(128)} %get-tuple-element.8.loglik), custom_call_target="tpu_custom_call" | custom-call | flops 6710886400 | bytes 16000000 | tf_op jit(solution)/shard_map/back/pallas_call | solution.py:433
